TPU v7x, 256 devices: a whole 4x4x8 slice. The times are simulated.
256 devices in a mesh: vir: 32 (over x, z), occ: 4 (over y), rep: 2 (over core).
Axes of the slice: x: 4, y: 4, z: 8, core: 2. Of those that a mesh axis runs over, the one named last changes fastest.
Arguments:
- amplitudes: float32 [256, 64, 4096], P('vir', ('occ', 'rep')), may hold values from -6 to 6
- integrals: float32 [384, 512, 4096], P('vir', None, ('occ', 'rep')), may hold values from -0.005859375 to 0.005859375
- block_owner: int32 [256], replicated, may hold values from 0 to 31, as said below
Outputs:
- ladder: float32 [64, 512], P('occ', 'rep')
Inputs may be any that keep to these rules, and one draw needn't show every extreme that they name: `block_owner`: blocks 8 * s to 8 * s + 7 start on vir index s. No vir index owns more than 12 blocks and some owns exactly 12; slots beyond an index's count are unused. No vir index's starting blocks name one owner more than 2 times, and each names some owner exactly 2 times.
All inputs are finite; a program needn't handle non-finite values.
Results may differ from a plain program's by a relative error of at most 0.0001.
Values sent between devices are 32-bit elements; how exact they have to be, the bound alone decides.
No kernel may reach another device: no remote copies, remote signals or barrier semaphores. Data moves between devices by JAX's collectives and lax.ppermute only.
A program may use at most 128 MiB of HBM per device.

v0:
```python
import jax
import jax.numpy as jnp
from jax import lax
from jax.sharding import PartitionSpec as P


def block_ranks(owners, blocks_dev):
    block_ids = jnp.arange(owners.shape[0], dtype=jnp.int32)
    earlier = block_ids[None, :] < block_ids[:, None]
    same_owner = owners[None, :] == owners[:, None]
    same_source = block_ids[None, :] // blocks_dev == block_ids[:, None] // blocks_dev
    owner_rank = jnp.sum(jnp.where(same_owner & earlier, 1, 0), axis=1).astype(jnp.int32)
    src_rank = jnp.sum(jnp.where(same_owner & earlier & same_source, 1, 0), axis=1).astype(
        jnp.int32
    )
    return (owner_rank, src_rank)


def contract(owned, integrals):
    return jnp.einsum(
        "vpx,vax->pa",
        owned,
        integrals,
        precision=lax.Precision.HIGHEST,
        preferred_element_type=jnp.float32,
    )


def on_device(amplitudes, integrals, block_owner):
    vir_count = lax.axis_size("vir")
    blocks_dev = amplitudes.shape[0]
    slot_count = integrals.shape[0]
    capacity = max(2, 3 * blocks_dev // (2 * vir_count))
    vir_index = lax.axis_index("vir")
    owner_rank, src_rank = block_ranks(block_owner, blocks_dev)
    block_ids = jnp.arange(block_owner.shape[0], dtype=jnp.int32)
    is_mine = block_owner == vir_index
    slot_pick = is_mine[None, :] & (
        owner_rank[None, :] == jnp.arange(slot_count, dtype=jnp.int32)[:, None]
    )
    slot_live = jnp.sum(jnp.where(slot_pick, 1, 0), axis=1)
    chosen = jnp.sum(jnp.where(slot_pick, block_ids[None, :], 0), axis=1)
    flat_index = chosen // blocks_dev * capacity + src_rank[chosen]
    slot_mask = slot_live.astype(jnp.float32)[:, None, None]
    local_ids = vir_index * blocks_dev + jnp.arange(blocks_dev, dtype=jnp.int32)
    target = block_owner[local_ids]
    target_rank = src_rank[local_ids]
    target_hit = (
        target[None, None, :] == jnp.arange(vir_count, dtype=jnp.int32)[:, None, None]
    ) & (target_rank[None, None, :] == jnp.arange(capacity, dtype=jnp.int32)[None, :, None])
    send_index = jnp.sum(
        jnp.where(target_hit, jnp.arange(blocks_dev, dtype=jnp.int32)[None, None, :], 0), axis=2
    )
    send_live = jnp.sum(jnp.where(target_hit, 1, 0), axis=2).astype(jnp.float32)
    outgoing = jnp.take(amplitudes, send_index, axis=0) * send_live[:, :, None, None]
    arrived = lax.all_to_all(outgoing, "vir", split_axis=0, concat_axis=0, tiled=True)
    row_stack = arrived.reshape((arrived.shape[0] * arrived.shape[1],) + arrived.shape[2:])
    owned = jnp.take(row_stack, flat_index, axis=0) * slot_mask
    owned = lax.all_to_all(owned, ("occ", "rep"), split_axis=2, concat_axis=1, tiled=True)
    partial_value = contract(owned, integrals)
    rep_part = lax.psum_scatter(partial_value, "rep", scatter_dimension=1, tiled=True)
    pair_part = lax.psum_scatter(rep_part, "occ", scatter_dimension=0, tiled=True)
    return lax.psum(pair_part, "vir")


def solution(mesh):
    in_specs = (P("vir", ("occ", "rep"), None), P("vir", None, ("occ", "rep")), P())
    out_specs = P("occ", "rep")
    return jax.shard_map(
        on_device, mesh=mesh, in_specs=in_specs, out_specs=out_specs, check_vma=False
    )
```

profile of v0, /device:TPU:0, one launch (start us, length us, event | category | flops | bytes accessed | tf_op | source)
XLA Modules:
  0.0 531.7 jit_solution(18139110158587541731)
XLA Ops:
  6.5 0.0 copy-start
  6.6 1.0 select_reduce_fusion.1
  7.6 1.3 gather_fusion.1
  8.9 0.6 gather_fusion.2
  9.6 0.1 iota_compare_fusion.2
  9.7 0.1 fusion.8
  9.8 0.1 copy.20
  9.9 0.1 reshape.278
  10.0 0.1 copy.19
  10.1 0.1 copy.21
  10.2 0.0 copy-done
  10.2 4.3 gather_fusion.3
  14.5 8.5 %select_multiply_fusion = f32[32,2,8,4096]{3,2,1,0:T(8,128)} fusion(f32[32,2,8,4096]{3,2,1,0:T(8,128)} %bitcast.42, f32[32,2]{1,0:T(8,128)S(1)} %copy.21, pred[32,2]{1,0:T(8,128)(4,1)S(1)} %copy.19), kind=kLoop, calls=%fused_computation.5 | loop fusion | flops 4194304 | bytes 16777536 | tf_op jit(solution)/shard_map/mul | solution.py:55
  22.9 0.0 copy-start.2
  22.9 9.8 %all-to-all-start = ((f32[32,2,8,4096]{3,2,1,0:T(8,128)}), f32[32,2,8,4096]{3,2,1,0:T(8,128)}, u32[]{:S(2)}, u32[]{:S(2)}) async-start(f32[32,2,8,4096]{3,2,1,0:T(8,128)} %select_multiply_fusion), calls=%async_computation | async-start | bytes 16777216 | tf_op jit(solution)/shard_map/all_to_all | solution.py:56
  32.8 0.0 reduce-scatter.3.cloned.1.call-start
  32.8 0.0 copy-done.2
  32.9 0.1 select_reduce_fusion.2
  33.0 0.7 gather_fusion
  33.7 187.9 %all-to-all-done = f32[32,2,8,4096]{3,2,1,0:T(8,128)} async-done(((f32[32,2,8,4096]{3,2,1,0:T(8,128)}), f32[32,2,8,4096]{3,2,1,0:T(8,128)}, u32[]{:S(2)}, u32[]{:S(2)}) %all-to-all-start) | async-done | bytes 8388640 | tf_op jit(solution)/shard_map/all_to_all | solution.py:56
  221.6 5.3 gather_fusion.4
  226.9 1.6 select_multiply_fusion.1
  228.5 9.0 %copy.22 = f32[12,8,4096]{0,1,2:T(8,128)} copy(f32[12,8,4096]{2,1,0:T(8,128)S(1)} %select_multiply_fusion.1) | data formatting | bytes 3145728 | tf_op jit(solution)/shard_map/mul | solution.py:58
  237.5 18.2 %reshape.294 = f32[8,1,49152]{2,1,0:T(1,128)S(1)} reshape(f32[4096,8,12]{2,1,0:T(8,128)} %bitcast.40) | data formatting | bytes 3145728
  255.7 26.2 %all_to_all.23 = f32[8,1,49152]{2,1,0:T(1,128)} all-to-all(f32[8,1,49152]{2,1,0:T(1,128)S(1)} %reshape.294), channel_id=1, replica_groups=mesh['vir'=32,'occ'=4,'rep'=2] {'occ','rep'}, dimensions={0} | all-to-all | bytes 3145728 | tf_op jit(solution)/shard_map/all_to_all | solution.py:59
  281.9 0.5 broadcast.330
  282.4 5.8 %reduce = f32[8,49152]{1,0:T(8,128)S(1)} reduce(f32[8,1,49152]{2,1,0:T(1,128)} %all_to_all.23, f32[]{:T(128)} %broadcast.330), dimensions={1}, to_apply=%all_to_all.17.reduce_sub_computation | reduce | bytes 3145732 | tf_op jit(solution)/shard_map/all_to_all | solution.py:59
  288.2 24.4 %reshape.295 = f32[4096,8,12]{2,1,0:T(8,128)} reshape(f32[8,49152]{1,0:T(8,128)S(1)} %reduce) | data formatting | bytes 3145728
  312.6 0.0 copy-start.1
  312.6 10.2 %copy.23 = f32[12,8,8,512]{3,1,2,0:T(8,128)S(1)} copy(f32[12,8,8,512]{0,1,3,2:T(8,128)} %bitcast.41) | data formatting | bytes 3145728 | tf_op jit(solution)/shard_map/all_to_all | solution.py:59
  322.8 15.7 %fusion.2 = f32[64,512]{1,0:T(8,128)} fusion(f32[12,512,512]{2,1,0:T(8,128)} %param.4, f32[12,8,8,512]{3,1,2,0:T(8,128)S(1)} %copy.23), kind=kOutput, calls=%fused_computation.9 | convolution fusion | flops 2415919104 | bytes 14286848 | tf_op jit(solution)/shard_map/vpx,vax->pa/dot_general | solution.py:20
  338.5 0.0 reduce-scatter.3.cloned.1.call-update
  338.5 0.0 reduce-scatter.5.cloned.1.call-start
  338.6 16.5 %reduce-scatter.3.cloned.1.call-done = f32[64,256]{1,0:T(8,128)} async-done(((f32[64,512]{1,0:T(8,128)}), f32[64,256]{1,0:T(8,128)}) %reduce-scatter.3.cloned.1.call-update) | async-done | bytes 65552 | tf_op jit(solution)/shard_map/reduce_scatter | solution.py:61
  355.1 0.0 reduce-scatter.5.cloned.1.call-update
  355.1 26.6 %reduce-scatter.5.cloned.1.call-done = f32[16,256]{1,0:T(8,128)} async-done(((f32[64,256]{1,0:T(8,128)}), f32[16,256]{1,0:T(8,128)}) %reduce-scatter.5.cloned.1.call-update) | async-done | bytes 16400 | tf_op jit(solution)/shard_map/reduce_scatter | solution.py:62
  381.8 143.1 %psum.7 = f32[16,256]{1,0:T(8,128)} all-reduce(f32[16,256]{1,0:T(8,128)} %reduce-scatter.5.cloned.1.call-done), channel_id=1, replica_groups=mesh['vir'=32,'occ'=4,'rep'=2] {'vir'}, use_global_device_ids=true, to_apply=%region_8.9 | all-reduce | flops 4096 | bytes 32768 | tf_op jit(solution)/shard_map/psum | solution.py:63
  524.9 0.0 copy-done.1
  (15 shorter events, 0.1 us)
Async XLA Ops:
  6.5 3.6 copy-start
  22.9 9.9 %copy-start.2 = (s32[256]{0:T(256)S(1)}, s32[256]{0:T(256)}, u32[]{:S(2)}) copy-start(s32[256]{0:T(256)} %param.5) | copy-start | bytes 3076
  22.9 198.6 %all-to-all-start = ((f32[32,2,8,4096]{3,2,1,0:T(8,128)}), f32[32,2,8,4096]{3,2,1,0:T(8,128)}, u32[]{:S(2)}, u32[]{:S(2)}) async-start(f32[32,2,8,4096]{3,2,1,0:T(8,128)} %select_multiply_fusion), calls=%async_computation | async-start | bytes 16777216 | tf_op jit(solution)/shard_map/all_to_all | solution.py:56
  32.8 322.3 %reduce-scatter.3.cloned.1.call-start = ((), (), s32[]{:S(2)}) async-start(), calls=%async_computation.4 | async-start | bytes 196608 | tf_op jit(solution)/shard_map/reduce_scatter | solution.py:61
  312.6 212.3 %copy-start.1 = (f32[8,8,4096]{2,1,0:T(8,128)S(1)}, f32[8,8,4096]{2,1,0:T(8,128)}, u32[]{:S(2)}) copy-start(f32[8,8,4096]{2,1,0:T(8,128)} %param.3) | copy-start | bytes 3145732
  338.5 43.3 %reduce-scatter.5.cloned.1.call-start = ((), (), s32[]{:S(2)}) async-start(), calls=%async_computation.5 | async-start | bytes 81920 | tf_op jit(solution)/shard_map/reduce_scatter | solution.py:62
Sparse Core Ops, SparseCore 0:
  338.7 16.4 reduce-scatter.2
  357.6 24.1 reduce-scatter.4
where the time goes:
time: 532 us
  waiting for transfers between devices  231 us (43%)
  blocking collectives  169 us (32%)
  local copies, waits for them, and re-layouts  74.9 us (14%)
  other arithmetic  17.3 us (3%)
  matrix products  15.7 us (3%)
  between operations  13.5 us (3%)
  starting transfers between devices  9.92 us (2%)
    all_to_all x1, waiting for transfers between devices, on_device(): lax.all_to_all(outgoing, 'vir', split_axis=0, concat_axis=0, tiled=True)  188 us
    psum x1, blocking collectives, on_device(): return lax.psum(pair_part, 'vir')  143 us
    unnamed x8, local copies, waits for them, and re-layouts  42.6 us
    reduce_scatter x1, waiting for transfers between devices, on_device(): lax.psum_scatter(rep_part, 'occ', scatter_dimension=0, tiled=True)  26.6 us
    all_to_all x1, blocking collectives, on_device(): lax.all_to_all(owned, ('occ', 'rep'), split_axis=2, concat_axis=1, tiled=...  26.2 us
    reduce_scatter x1, waiting for transfers between devices, on_device(): lax.psum_scatter(partial_value, 'rep', scatter_dimension=1, tiled=True)  16.5 us
    dot_general x1, matrix products, contract(): jnp.einsum('vpx,vax->pa', owned, integrals, precision=lax.Precision.HIGHE...  15.7 us
    all_to_all x2, local copies, waits for them, and re-layouts, on_device(): lax.all_to_all(owned, ('occ', 'rep'), split_axis=2, concat_axis=1, tiled=...  10.7 us
  transfers between devices with their start and end apart: 3, of which 3 were waited for; matrix products, arithmetic and copies ran while one was open for 0% of the time, Pallas kernels for 0%

commit v1 on v0

--- a/solution.py
+++ b/solution.py
@@ -56,7 +56,15 @@
     arrived = lax.all_to_all(outgoing, "vir", split_axis=0, concat_axis=0, tiled=True)
     row_stack = arrived.reshape((arrived.shape[0] * arrived.shape[1],) + arrived.shape[2:])
     owned = jnp.take(row_stack, flat_index, axis=0) * slot_mask
-    owned = lax.all_to_all(owned, ("occ", "rep"), split_axis=2, concat_axis=1, tiled=True)
+    ways, here = (lax.axis_size(("occ", "rep")), lax.axis_index(("occ", "rep")))
+    width = owned.shape[2] // ways
+    turned = jnp.roll(owned, -here * width, axis=2)
+    got = [lax.slice_in_dim(turned, 0, width, axis=2)]
+    for far in range(1, ways):
+        sent = lax.slice_in_dim(turned, far * width, (far + 1) * width, axis=2)
+        got.append(lax.ppermute(sent, ("occ", "rep"), [(d, (d + far) % ways) for d in range(ways)]))
+    line = jnp.concatenate(got[::-1], axis=1)
+    owned = jnp.roll(line, (here + 1) * got[0].shape[1], axis=1)
     partial_value = contract(owned, integrals)
     rep_part = lax.psum_scatter(partial_value, "rep", scatter_dimension=1, tiled=True)
     pair_part = lax.psum_scatter(rep_part, "occ", scatter_dimension=0, tiled=True)

time: 532 us -> 461 us (0.87)
  local copies, waits for them, and re-layouts: 74.9 us -> 12.6 us
  blocking collectives: 169 us -> 143 us
  waiting for transfers between devices: 231 us -> 248 us
  starting transfers between devices: 9.92 us -> 17.1 us
  other arithmetic: 17.3 us -> 10.4 us
    unnamed x8 -> x19, local copies, waits for them, and re-layouts: 42.6 us -> 0.23 us
    all_to_all x1 -> x0, blocking collectives: 26.2 us -> none  [on_device(): lax.all_to_all(owned, ('occ', 'rep'), split_axis=2, concat_axis=1, tiled=...]
    ppermute x0 -> x7, waiting for transfers between devices: none -> 17.7 us  [on_device(): lax.ppermute(sent, ('occ', 'rep'), [(d, (d + far) % ways) for d in range(...]
    all_to_all x2 -> x0, local copies, waits for them, and re-layouts: 10.7 us -> none  [on_device(): lax.all_to_all(owned, ('occ', 'rep'), split_axis=2, concat_axis=1, tiled=...]
    mul x1 -> x0, local copies, waits for them, and re-layouts: 9.02 us -> none  [on_device(): owned = jnp.take(row_stack, flat_index, axis=0) * slot_mask]
    ppermute x0 -> x7, starting transfers between devices: none -> 7.19 us  [on_device(): lax.ppermute(sent, ('occ', 'rep'), [(d, (d + far) % ways) for d in range(...]
    all_to_all x1 -> x0, other arithmetic: 5.79 us -> none  [on_device(): lax.all_to_all(owned, ('occ', 'rep'), split_axis=2, concat_axis=1, tiled=...]
  transfers between devices with their start and end apart: 3 -> 10, of which waited for: 3 -> 8; matrix products, arithmetic and copies ran while one was open for 0% -> 0% of each run, Pallas kernels for 0% -> 0%
where the time goes in v1:
time: 461 us
  waiting for transfers between devices  248 us (54%)
  blocking collectives  143 us (31%)
  starting transfers between devices  17.1 us (4%)
  matrix products  15.7 us (3%)
  between operations  13.7 us (3%)
  local copies, waits for them, and re-layouts  12.6 us (3%)
  other arithmetic  10.4 us (2%)
    all_to_all x1, waiting for transfers between devices, on_device(): lax.all_to_all(outgoing, 'vir', split_axis=0, concat_axis=0, tiled=True)  188 us
    psum x1, blocking collectives, on_device(): return lax.psum(pair_part, 'vir')  143 us
    reduce_scatter x1, waiting for transfers between devices, on_device(): lax.psum_scatter(rep_part, 'occ', scatter_dimension=0, tiled=True)  26.6 us
    ppermute x7, waiting for transfers between devices, on_device(): lax.ppermute(sent, ('occ', 'rep'), [(d, (d + far) % ways) for d in range(...  17.7 us
    reduce_scatter x1, waiting for transfers between devices, on_device(): lax.psum_scatter(partial_value, 'rep', scatter_dimension=1, tiled=True)  16 us
    dot_general x1, matrix products, contract(): jnp.einsum('vpx,vax->pa', owned, integrals, precision=lax.Precision.HIGHE...  15.7 us
    all_to_all x1, starting transfers between devices, on_device(): lax.all_to_all(outgoing, 'vir', split_axis=0, concat_axis=0, tiled=True)  9.84 us
  transfers between devices with their start and end apart: 10, of which 8 were waited for; matrix products, arithmetic and copies ran while one was open for 0% of the time, Pallas kernels for 0%

profile of v1, /device:TPU:0, one launch (start us, length us, event | category | flops | bytes accessed | tf_op | source)
XLA Modules:
  0.0 460.8 jit_solution(3068517954660464515)
XLA Ops:
  6.5 0.0 copy-start
  6.6 1.0 select_reduce_fusion.1
  7.6 1.3 gather_fusion.1
  8.9 0.6 gather_fusion.2
  9.6 0.1 iota_compare_fusion.2
  9.7 0.1 fusion.9
  9.8 0.1 copy.9
  9.9 0.1 reshape.278
  10.0 0.1 copy.8
  10.1 0.1 copy.10
  10.2 0.0 copy-done
  10.2 4.3 gather_fusion.3
  14.5 8.5 %select_multiply_fusion = f32[32,2,8,4096]{3,2,1,0:T(8,128)} fusion(f32[32,2,8,4096]{3,2,1,0:T(8,128)} %bitcast.30, f32[32,2]{1,0:T(8,128)S(1)} %copy.10, pred[32,2]{1,0:T(8,128)(4,1)S(1)} %copy.8), kind=kLoop, calls=%fused_computation.5 | loop fusion | flops 4194304 | bytes 16777536 | tf_op jit(solution)/shard_map/mul | solution.py:55
  22.9 0.0 copy-start.1
  22.9 9.8 %all-to-all-start = ((f32[32,2,8,4096]{3,2,1,0:T(8,128)}), f32[32,2,8,4096]{3,2,1,0:T(8,128)}, u32[]{:S(2)}, u32[]{:S(2)}) async-start(f32[32,2,8,4096]{3,2,1,0:T(8,128)} %select_multiply_fusion), calls=%async_computation | async-start | bytes 16777216 | tf_op jit(solution)/shard_map/all_to_all | solution.py:56
  32.8 0.0 reduce-scatter.3.cloned.1.call-start
  32.9 0.0 copy-done.1
  32.9 0.1 select_reduce_fusion.2
  33.0 0.7 gather_fusion
  33.8 187.8 %all-to-all-done = f32[32,2,8,4096]{3,2,1,0:T(8,128)} async-done(((f32[32,2,8,4096]{3,2,1,0:T(8,128)}), f32[32,2,8,4096]{3,2,1,0:T(8,128)}, u32[]{:S(2)}, u32[]{:S(2)}) %all-to-all-start) | async-done | bytes 8388640 | tf_op jit(solution)/shard_map/all_to_all | solution.py:56
  221.6 4.0 gather_fusion.4
  225.6 0.2 select_multiply_fusion.1
  225.8 0.3 fusion
  226.2 1.0 fusion.14
  227.2 1.6 collective-permute-start
  228.7 1.4 collective-permute-start.1
  230.2 0.5 collective-permute-start.2
  230.6 2.9 collective-permute-start.3
  233.5 0.0 collective-permute-start.4
  233.5 0.0 collective-permute-done
  233.5 0.8 collective-permute-start.5
  234.4 4.5 collective-permute-done.1
  238.9 0.0 collective-permute-start.6
  238.9 0.0 collective-permute-done.2
  239.0 4.8 %collective-permute-done.3 = f32[12,8,512]{2,1,0:T(8,128)S(1)} collective-permute-done((f32[12,8,512]{2,1,0:T(8,128)}, f32[12,8,512]{2,1,0:T(8,128)S(1)}, u32[]{:S(2)}, u32[]{:S(2)}) %collective-permute-start.3) | collective-permute-done | bytes 196640 | tf_op jit(solution)/shard_map/ppermute | solution.py:65
  243.7 0.1 collective-permute-done.4
  243.9 8.2 %collective-permute-done.5 = f32[12,8,512]{2,1,0:T(8,128)S(1)} collective-permute-done((f32[12,8,512]{2,1,0:T(8,128)S(1)}, f32[12,8,512]{2,1,0:T(8,128)S(1)}, u32[]{:S(2)}, u32[]{:S(2)}) %collective-permute-start.5) | collective-permute-done | bytes 196640 | tf_op jit(solution)/shard_map/ppermute | solution.py:65
  252.1 0.1 collective-permute-done.6
  252.4 15.7 %fusion.3 = f32[64,512]{1,0:T(8,128)} fusion(f32[12,512,512]{2,1,0:T(8,128)} %param.4, f32[12,128,512]{2,1,0:T(8,128)S(1)} %slice_dynamic-update-slice_fusion.1, s32[]{:T(128)S(6)} %select_n.160), kind=kOutput, calls=%fused_computation.12 | convolution fusion | flops 2415919104 | bytes 14286852 | tf_op jit(solution)/shard_map/vpx,vax->pa/dot_general | solution.py:20
  268.1 0.0 reduce-scatter.3.cloned.1.call-update
  268.1 0.0 reduce-scatter.5.cloned.1.call-start
  268.2 16.0 %reduce-scatter.3.cloned.1.call-done = f32[64,256]{1,0:T(8,128)} async-done(((f32[64,512]{1,0:T(8,128)}), f32[64,256]{1,0:T(8,128)}) %reduce-scatter.3.cloned.1.call-update) | async-done | bytes 65552 | tf_op jit(solution)/shard_map/reduce_scatter | solution.py:69
  284.2 0.0 reduce-scatter.5.cloned.1.call-update
  284.2 26.6 %reduce-scatter.5.cloned.1.call-done = f32[16,256]{1,0:T(8,128)} async-done(((f32[64,256]{1,0:T(8,128)}), f32[16,256]{1,0:T(8,128)}) %reduce-scatter.5.cloned.1.call-update) | async-done | bytes 16400 | tf_op jit(solution)/shard_map/reduce_scatter | solution.py:70
  310.8 143.1 %psum.7 = f32[16,256]{1,0:T(8,128)} all-reduce(f32[16,256]{1,0:T(8,128)} %reduce-scatter.5.cloned.1.call-done), channel_id=1, replica_groups=mesh['vir'=32,'occ'=4,'rep'=2] {'vir'}, use_global_device_ids=true, to_apply=%region_8.9 | all-reduce | flops 4096 | bytes 32768 | tf_op jit(solution)/shard_map/psum | solution.py:71
  (31 shorter events, 0.4 us)
Async XLA Ops:
  6.5 3.6 copy-start
  22.9 9.9 %copy-start.1 = (s32[256]{0:T(256)S(1)}, s32[256]{0:T(256)}, u32[]{:S(2)}) copy-start(s32[256]{0:T(256)} %param.5) | copy-start | bytes 3076
  22.9 198.6 %all-to-all-start = ((f32[32,2,8,4096]{3,2,1,0:T(8,128)}), f32[32,2,8,4096]{3,2,1,0:T(8,128)}, u32[]{:S(2)}, u32[]{:S(2)}) async-start(f32[32,2,8,4096]{3,2,1,0:T(8,128)} %select_multiply_fusion), calls=%async_computation | async-start | bytes 16777216 | tf_op jit(solution)/shard_map/all_to_all | solution.py:56
  32.8 251.4 %reduce-scatter.3.cloned.1.call-start = ((), (), s32[]{:S(2)}) async-start(), calls=%async_computation.3 | async-start | bytes 196608 | tf_op jit(solution)/shard_map/reduce_scatter | solution.py:69
  227.2 6.4 %collective-permute-start = (f32[12,8,512]{2,1,0:T(8,128)}, f32[12,8,512]{2,1,0:T(8,128)S(1)}, u32[]{:S(2)}, u32[]{:S(2)}) collective-permute-start(f32[12,8,512]{2,1,0:T(8,128)} %get-tuple-element.17), channel_id=1, source_target_pairs={{0,7},{1,0},{2,1},{3,2},{4,3},{5,4},{6,5},{7,6},{8,15},{9,8},{10,9... | collective-permute-start | bytes 589832 | tf_op jit(solution)/shard_map/ppermute | solution.py:65
  228.7 10.2 %collective-permute-start.1 = (f32[12,8,512]{2,1,0:T(8,128)}, f32[12,8,512]{2,1,0:T(8,128)S(1)}, u32[]{:S(2)}, u32[]{:S(2)}) collective-permute-start(f32[12,8,512]{2,1,0:T(8,128)} %get-tuple-element.16), channel_id=1, source_target_pairs={{0,6},{1,7},{2,0},{3,1},{4,2},{5,3},{6,4},{7,5},{8,14},{9,15},{10,... | collective-permute-start | bytes 589832 | tf_op jit(solution)/shard_map/ppermute | solution.py:65
  230.2 8.8 %collective-permute-start.2 = (f32[12,8,512]{2,1,0:T(8,128)}, f32[12,8,512]{2,1,0:T(8,128)S(1)}, u32[]{:S(2)}, u32[]{:S(2)}) collective-permute-start(f32[12,8,512]{2,1,0:T(8,128)} %get-tuple-element.15), channel_id=1, source_target_pairs={{0,5},{1,6},{2,7},{3,0},{4,1},{5,2},{6,3},{7,4},{8,13},{9,14},{10,... | collective-permute-start | bytes 589832 | tf_op jit(solution)/shard_map/ppermute | solution.py:65
  230.6 13.1 %collective-permute-start.3 = (f32[12,8,512]{2,1,0:T(8,128)}, f32[12,8,512]{2,1,0:T(8,128)S(1)}, u32[]{:S(2)}, u32[]{:S(2)}) collective-permute-start(f32[12,8,512]{2,1,0:T(8,128)} %get-tuple-element.14), channel_id=1, source_target_pairs={{0,4},{1,5},{2,6},{3,7},{4,0},{5,1},{6,2},{7,3},{8,12},{9,13},{10,... | collective-permute-start | bytes 589832 | tf_op jit(solution)/shard_map/ppermute | solution.py:65
  233.5 10.3 %collective-permute-start.4 = (f32[12,8,512]{2,1,0:T(8,128)}, f32[12,8,512]{2,1,0:T(8,128)S(1)}, u32[]{:S(2)}, u32[]{:S(2)}) collective-permute-start(f32[12,8,512]{2,1,0:T(8,128)} %get-tuple-element.13), channel_id=1, source_target_pairs={{0,3},{1,4},{2,5},{3,6},{4,7},{5,0},{6,1},{7,2},{8,11},{9,12},{10,... | collective-permute-start | bytes 589832 | tf_op jit(solution)/shard_map/ppermute | solution.py:65
  233.5 18.5 %collective-permute-start.5 = (f32[12,8,512]{2,1,0:T(8,128)S(1)}, f32[12,8,512]{2,1,0:T(8,128)S(1)}, u32[]{:S(2)}, u32[]{:S(2)}) collective-permute-start(f32[12,8,512]{2,1,0:T(8,128)S(1)} %get-tuple-element.12), channel_id=1, source_target_pairs={{0,2},{1,3},{2,4},{3,5},{4,6},{5,7},{6,0},{7,1},{8,10},{9,11},{10,... | collective-permute-start | bytes 589832 | tf_op jit(solution)/shard_map/ppermute | solution.py:65
  238.9 13.2 %collective-permute-start.6 = (f32[12,8,512]{2,1,0:T(8,128)S(1)}, f32[12,8,512]{2,1,0:T(8,128)S(1)}, u32[]{:S(2)}, u32[]{:S(2)}) collective-permute-start(f32[12,8,512]{2,1,0:T(8,128)S(1)} %get-tuple-element.11), channel_id=1, source_target_pairs={{0,1},{1,2},{2,3},{3,4},{4,5},{5,6},{6,7},{7,0},{8,9},{9,10},{10,1... | collective-permute-start | bytes 589832 | tf_op jit(solution)/shard_map/ppermute | solution.py:65
  268.1 42.7 %reduce-scatter.5.cloned.1.call-start = ((), (), s32[]{:S(2)}) async-start(), calls=%async_computation.4 | async-start | bytes 81920 | tf_op jit(solution)/shard_map/reduce_scatter | solution.py:70
Sparse Core Ops, SparseCore 0:
  268.2 15.8 reduce-scatter.2
  286.7 24.1 reduce-scatter.4
